TPU v7x, 512 devices: a whole 4x4x16 slice. The times are simulated.
512 devices in a mesh: date: 16 (over z_hi, x, core), band: 32 (over z_lo, y).
Axes of the slice: x: 4, y: 4, z: 16 (z_hi: 2, z_lo: 8; z = z_hi * 8 + z_lo), core: 2. Of those that a mesh axis runs over, the one named last changes fastest.
Arguments:
- model_prognosis: bfloat16 [32, 2, 5, 128, 360], P('date', None, None, 'band'), may hold values from -6 to 6
- analysis_truth: bfloat16 [32, 2, 5, 512, 1440], P('date', None, None, 'band'), may hold values from -6 to 6
- expected_normal: bfloat16 [2, 5, 512, 1440], P(None, None, 'band'), may hold values from -5 to 5
- parallel_first_indices: int32 [512], P('band'), may hold values from -2 to 126, as said below
- parallel_blend_factors: float32 [512, 4], P('band'), may hold values from 0.05 to 0.5
- meridian_first_indices: int32 [1440], replicated, may hold values from 0 to 359, as said below
- meridian_blend_factors: bfloat16 [4, 1440], replicated, may hold values from 0.049804688 to 0.5
Outputs:
- sq_error: float32 [2, 5, 512, 1440], P(None, None, ('band', 'date'))
- anom_product: float32 [2, 5, 512, 1440], P(None, None, ('band', 'date'))
Inputs may be any that keep to these rules, and one draw needn't show every extreme that they name: `parallel_first_indices`: fine row r's stencil starts at coarse row r // 4 - 2 or r // 4 - 1. `meridian_first_indices`: fine longitude x's stencil starts at coarse longitude (x // 4 - 1) or (x // 4), taken modulo 360.
All inputs are finite; a program needn't handle non-finite values.
Results may differ from a plain program's by a relative error of at most 0.0015.
Values may be sent and summed in bfloat16 or wider, within the bound.
A program may use at most 64 MiB of HBM per device.

v0:
```python
import jax
import jax.numpy as jnp
from jax import lax
from jax.sharding import PartitionSpec as P


def padded(block, sides, width):
    for axis, dim in sides:
        count = lax.axis_size(axis)
        forward = [(i, i + 1) for i in range(count - 1)]
        backward = [(target, source) for source, target in forward]
        low = lax.ppermute(
            lax.slice_in_dim(block, block.shape[dim] - width, None, axis=dim), axis, forward
        )
        high = lax.ppermute(lax.slice_in_dim(block, 0, width, axis=dim), axis, backward)
        block = jnp.concatenate([low, block, high], axis=dim)
    return block


def lon_table(meridian_first_indices, meridian_blend_factors, sparse_easting_number):
    columns = jnp.arange(sparse_easting_number, dtype=jnp.int32)[:, None]
    weights = meridian_blend_factors.astype(jnp.float32)
    table = jnp.zeros((sparse_easting_number, meridian_first_indices.shape[0]), jnp.float32)
    for stencil in range(4):
        target = ((meridian_first_indices + stencil) % sparse_easting_number)[None, :]
        table = table + weights[stencil][None, :] * (columns == target).astype(jnp.float32)
    return table.astype(jnp.bfloat16)


def shards(
    model_prognosis,
    analysis_truth,
    expected_normal,
    parallel_first_indices,
    parallel_blend_factors,
    meridian_first_indices,
    meridian_blend_factors,
):
    init_date_count, lead_time_count, variable_count, coarse_row_count, sparse_easting_number = (
        model_prognosis.shape
    )
    fine_rows = analysis_truth.shape[3]
    dense_easting_extent = analysis_truth.shape[4]
    table = lon_table(meridian_first_indices, meridian_blend_factors, sparse_easting_number)
    enlarged_prognosis_arrays = padded(model_prognosis, (("band", 3),), 2)
    flattened_arrays = enlarged_prognosis_arrays.reshape(-1, sparse_easting_number)
    returned_pair = jnp.dot(flattened_arrays, table, preferred_element_type=jnp.float32)
    through_axis = returned_pair.reshape(
        enlarged_prognosis_arrays.shape[:-1] + (dense_easting_extent,)
    )
    first_row = lax.axis_index("band") * coarse_row_count - 2
    local_start = parallel_first_indices - first_row
    columns = jnp.arange(coarse_row_count + 4, dtype=jnp.int32)[None, :]
    lat_table = jnp.zeros((fine_rows, coarse_row_count + 4), jnp.float32)
    for stencil in range(4):
        lat_table = lat_table + parallel_blend_factors[:, stencil][:, None] * (
            columns == (local_start + stencil)[:, None]
        ).astype(jnp.float32)
    climate_all = expected_normal.astype(jnp.float32)
    fine = jnp.einsum("rc,dlvcx->dlvrx", lat_table, through_axis, precision=lax.Precision.HIGHEST)
    actual = analysis_truth.astype(jnp.float32)
    error_map = fine - actual
    fcst_anom = fine - climate_all
    true_anom = actual - climate_all
    terms = jnp.stack(
        [jnp.sum(error_map * error_map, axis=0), jnp.sum(fcst_anom * true_anom, axis=0)], axis=0
    )
    partial_maps = jnp.moveaxis(terms, 3, 0)
    total = lax.psum_scatter(partial_maps, "date", scatter_dimension=0, tiled=True)
    total = total / (init_date_count * lax.axis_size("date"))
    sq_error = jnp.transpose(total[:, 0], (1, 2, 0, 3))
    anom_product = jnp.transpose(total[:, 1], (1, 2, 0, 3))
    return (sq_error, anom_product)


def solution(mesh):
    in_specs = (
        P("date", None, None, "band", None),
        P("date", None, None, "band", None),
        P(None, None, "band", None),
        P("band"),
        P("band", None),
        P(),
        P(),
    )
    out_specs = (P(None, None, ("band", "date"), None), P(None, None, ("band", "date"), None))
    return jax.shard_map(shards, mesh=mesh, in_specs=in_specs, out_specs=out_specs, check_vma=False)
```

profile of v0, /device:TPU:1, one launch (start us, length us, event | category | flops | bytes accessed | tf_op | source)
XLA Modules:
  0.0 177.2 jit_solution(17308805635721544664)
XLA Ops:
  7.2 0.0 reduce-scatter.2.cloned.1.call-start
  7.2 1.0 fusion.41
  8.2 4.0 %collective-permute-start = (bf16[2,2,5,2,360]{4,3,2,1,0:T(2,128)(2,1)S(1)}, bf16[2,2,5,2,360]{4,3,2,1,0:T(2,128)(2,1)S(1)}, u32[]{:S(2)}, u32[]{:S(2)}) collective-permute-start(bf16[2,2,5,2,360]{4,3,2,1,0:T(2,128)(2,1)S(1)} %get-tuple-element.16), channel_id=1, source_target_pairs={{0,1},{1,2},{2,3},{3,4},{4,5},{5,6},{6,7},{7,8},{8,9},{9,10},{10,1... | collective-permute-start | bytes 86408 | tf_op jit(solution)/shard_map/ppermute | solution.py:12
  12.2 1.3 collective-permute-start.1
  13.5 0.7 broadcast_add_fusion.2
  14.2 0.8 slice_bitcast_fusion.5
  15.0 0.7 convert_element_type.8
  15.7 0.7 add_select_fusion.3
  16.5 0.1 slice_reduce_fusion.3
  16.5 1.1 convert_element_type.11
  17.7 0.0 collective-permute-done
  17.7 0.0 collective-permute-done.1
  17.7 0.0 copy-start
  17.7 2.3 %fusion.5 = f32[2,2,5,8,1440]{4,3,2,1,0:T(8,128)S(1)} fusion(f32[1440]{0:T(1024)S(1)} %get-tuple-element.9, s32[1440]{0:T(1024)S(1)} %get-tuple-element.20, f32[1440]{0:T(1024)S(1)} %get-tuple-element.10, s32[1440]{0:T(1024)S(1)} %get-tuple-element.21, f32[1440]{0:T(1024)S(1)} %get-tuple-element.11, s32[1440]{0:T(1024)S(1)} %get-tuple-element.19, ...), kind=kOutput, calls=%fused_computation.14 | convolution fusion | flops 172454400 | bytes 1082880 | tf_op jit(solution)/shard_map/dot_general | solution.py:47
  20.0 0.0 copy-done
  20.0 2.2 %fusion.1 = (f32[2,5,16,1440]{3,2,1,0:T(8,128)S(1)}, f32[2,5,16,1440]{3,2,1,0:T(8,128)S(1)}) fusion(bf16[2,2,5,16,1440]{4,3,2,1,0:T(8,128)(2,1)S(1)} %copy-done, f32[2,5,16,1440]{3,2,1,0:T(8,128)S(1)} %convert_element_type.11, f32[2,2,5,8,1440]{4,3,2,1,0:T(8,128)S(1)} %fusion.5, f32[16]{0:T(128)S(1)} %get-tuple-element.24, s32[16]{0:T(128)S(1)} %get-tuple-element.27, ...), kind=kOutput, calls=%fused_computation.9 | convolution fusion | flops 47463808 | bytes 4608512 | tf_op jit(solution)/shard_map/rc,dlvcx->dlvrx/dot_general | solution.py:60
  22.2 0.2 maximum_bitcast_fusion
  22.4 2.9 %copy.11 = f32[16,2,2,5,1440]{4,3,2,1,0:T(8,128)} copy(f32[16,2,2,5,1440]{4,0,3,2,1:T(8,128)S(1)} %maximum_bitcast_fusion) | data formatting | bytes 3686400 | tf_op jit(solution)/shard_map/transpose | solution.py:68
  25.3 0.0 reduce-scatter.2.cloned.1.call-update
  25.3 142.7 %reduce-scatter.2.cloned.1.call-done = f32[1,2,2,5,1440]{4,3,2,1,0:T(8,128)} async-done(((f32[16,2,2,5,1440]{4,3,2,1,0:T(8,128)}), f32[1,2,2,5,1440]{4,3,2,1,0:T(8,128)}) %reduce-scatter.2.cloned.1.call-update) | async-done | bytes 115216 | tf_op jit(solution)/shard_map/reduce_scatter | solution.py:69
  168.0 0.9 broadcast_multiply_fusion
  169.0 0.7 copy.13
  169.7 0.7 copy.12
  (2 shorter events, 0.0 us)
Async XLA Ops:
  7.2 160.9 %reduce-scatter.2.cloned.1.call-start = ((), (), s32[]{:S(2)}) async-start(), calls=%async_computation.1 | async-start | bytes 3342336 | tf_op jit(solution)/shard_map/reduce_scatter | solution.py:69
  8.2 9.5 %collective-permute-start = (bf16[2,2,5,2,360]{4,3,2,1,0:T(2,128)(2,1)S(1)}, bf16[2,2,5,2,360]{4,3,2,1,0:T(2,128)(2,1)S(1)}, u32[]{:S(2)}, u32[]{:S(2)}) collective-permute-start(bf16[2,2,5,2,360]{4,3,2,1,0:T(2,128)(2,1)S(1)} %get-tuple-element.16), channel_id=1, source_target_pairs={{0,1},{1,2},{2,3},{3,4},{4,5},{5,6},{6,7},{7,8},{8,9},{9,10},{10,1... | collective-permute-start | bytes 86408 | tf_op jit(solution)/shard_map/ppermute | solution.py:12
  12.2 5.5 %collective-permute-start.1 = (bf16[2,2,5,2,360]{4,3,2,1,0:T(2,128)(2,1)S(1)}, bf16[2,2,5,2,360]{4,3,2,1,0:T(2,128)(2,1)S(1)}, u32[]{:S(2)}, u32[]{:S(2)}) collective-permute-start(bf16[2,2,5,2,360]{4,3,2,1,0:T(2,128)(2,1)S(1)} %get-tuple-element.17), channel_id=1, source_target_pairs={{1,0},{2,1},{3,2},{4,3},{5,4},{6,5},{7,6},{8,7},{9,8},{10,9},{11,1... | collective-permute-start | bytes 86408 | tf_op jit(solution)/shard_map/ppermute | solution.py:15
  17.7 2.3 %copy-start = (bf16[2,2,5,16,1440]{4,3,2,1,0:T(8,128)(2,1)S(1)}, bf16[2,2,5,16,1440]{4,3,2,1,0:T(8,128)(2,1)}, u32[]{:S(2)}) copy-start(bf16[2,2,5,16,1440]{4,3,2,1,0:T(8,128)(2,1)} %param.8) | copy-start | bytes 2764804
Sparse Core Ops, SparseCore 0:
  25.4 142.5 reduce-scatter.1
where the time goes:
time: 178 us; the launch traced here: 177 us
  waiting for transfers between devices  143 us (80%)
  between operations  14.1 us (8%)
  local copies, waits for them, and re-layouts  6.14 us (3%)
  starting transfers between devices  5.36 us (3%)
  matrix products  4.49 us (3%)
  other arithmetic  4.35 us (2%)
    reduce_scatter x1, waiting for transfers between devices, shards(): lax.psum_scatter(partial_maps, 'date', scatter_dimension=0, tiled=True)  143 us
    ppermute x1, starting transfers between devices, padded(): lax.ppermute(lax.slice_in_dim(block, block.shape[dim] - width, None, axis...  4.03 us
  transfers between devices with their start and end apart: 3, of which 1 were waited for; matrix products, arithmetic and copies ran while one was open for 2% of the time, Pallas kernels for 0%

commit v1 on v0

v1 whole, which is shorter than its diff:
```python
import functools

import jax
import jax.numpy as jnp
from jax import lax
from jax.experimental import pallas as pl
from jax.experimental.pallas import tpu as pltpu
from jax.sharding import PartitionSpec as P

MESH = pl.DeviceIdType.MESH
F32 = jnp.float32
BF16 = jnp.bfloat16
WIDE = 1440
COARSE = 360
CHUNK = 512
CHUNKS = 3


def kernel(
    model, truth, climate, starts, lat_w, lon_first, lon_w,
    out,
    tbuf, cbuf, crs, fields, table, pick, pick_c, xsend, xrecv, zsend, zown, zrecv,
    lsem, tsem, csend, crecv, xssem, xrsem, zssem, zrsem,
):
    date = lax.axis_index("date")
    band = lax.axis_index("band")
    bands = 32
    half = date // 8
    x = (date // 2) % 4
    core = date % 2

    def at(h, xx, c):
        return h * 8 + xx * 2 + c

    sibling = (at(half, x, 1 - core), band)
    across = [(at(half, (x + k) % 4, core), band) for k in (1, 2, 3)]
    far = (at(1 - half, x, core), band)
    up, down = (band + 1) % bands, (band + bands - 1) % bands
    near = [(date, up), (date, down), (at(half, x, 1 - core), up), (at(half, x, 1 - core), down)]
    barrier = pltpu.get_barrier_semaphore()
    for partner in [far, sibling] + near + across:
        pl.semaphore_signal(barrier, inc=1, device_id=partner, device_id_type=MESH)

    own_truth = pltpu.make_async_copy(truth, tbuf.at[0], lsem.at[0])
    own_truth.start()
    own_climate = pltpu.make_async_copy(climate, cbuf, lsem.at[1])
    own_climate.start()

    crs[0, 1:3] = jnp.zeros((2, 48, 384), BF16)
    m = model[...].astype(F32)
    for pair in range(2):
        rows = []
        for k in (2 * pair, 2 * pair + 1):
            plane = m[:, k, :]
            rows += [plane[0:8], plane[10:18]]
            a, b = plane[8:10], plane[18:20]
            rows += [a, a, b, b]
        crs[0, 1 + pair, :, 0:COARSE] = jnp.concatenate(rows, axis=0).astype(BF16)

    pl.semaphore_wait(barrier, 9)

    def send(src, dst, ssem, rsem, device):
        copy = pltpu.make_async_remote_copy(
            src_ref=src, dst_ref=dst, send_sem=ssem, recv_sem=rsem, device_id=device, device_id_type=MESH
        )
        copy.start()
        return copy

    coarse = [
        send(crs.at[0, 2], crs.at[0, 0], csend.at[0], crecv.at[0], near[0]),
        send(crs.at[0, 1], crs.at[0, 3], csend.at[1], crecv.at[1], near[1]),
        send(crs.at[0, 2], crs.at[1, 0], csend.at[2], crecv.at[2], near[2]),
        send(crs.at[0, 1], crs.at[1, 3], csend.at[3], crecv.at[3], near[3]),
        send(crs.at[0, pl.ds(1, 2)], crs.at[1, pl.ds(1, 2)], csend.at[4], crecv.at[4], sibling),
    ]
    other_truth = send(truth, tbuf.at[1], tsem.at[0], tsem.at[1], sibling)

    first_all = lon_first[...]
    weights_all = lon_w[...].astype(F32)
    for start in range(0, WIDE, CHUNK):
        width = min(CHUNK, WIDE - start)
        first = first_all[:, start : start + width]
        step = lax.broadcasted_iota(jnp.int32, (384, width), 0) - first
        step = jnp.where(step < 0, step + COARSE, step)
        block = jnp.zeros((384, width), F32)
        for k in range(4):
            block = jnp.where(step == k, weights_all[k : k + 1, start : start + width], block)
        row = lax.broadcasted_iota(jnp.int32, (384, width), 0)
        table[:, start : start + width] = jnp.where(row < COARSE, block, 0.0).astype(BF16)

    row = lax.broadcasted_iota(jnp.int32, (160, 1), 0)
    q = row - 128
    main = row < 128
    d_of = jnp.where(main, row // 64, (q % 8) // 4)
    x_of = jnp.where(main, (row % 64) // 16, q // 8)
    z_of = jnp.where(main, (row // 8) % 2, (q // 2) % 2)
    v_of = jnp.where(main, row % 8, 8 + q % 2)
    target = v_of * 16 + 8 * z_of + 2 * x_of + core
    column = lax.broadcasted_iota(jnp.int32, (160, 160), 1)
    pick_c[...] = (column == target).astype(F32).astype(BF16)
    column = lax.broadcasted_iota(jnp.int32, (160, 320), 1)
    pick[...] = (column == d_of * 160 + target).astype(F32).astype(BF16)
    xsend[:, CHUNKS - 1, :, 384:512] = jnp.zeros((4, 40, 128), F32)

    stencil = {}
    for xx in range(4):
        for z in range(2):
            r = 8 * z + 2 * xx + core
            base = 2 * z + xx // 2
            late = starts[r] - (4 * band + base - 2)
            w = [lat_w[k, r] for k in range(4)]
            five = [jnp.where(late == 0, w[0], 0.0)]
            five += [jnp.where(late == 0, w[j], w[j - 1]) for j in (1, 2, 3)]
            five += [jnp.where(late == 0, 0.0, w[3])]
            for j in range(5):
                value = five[j]
                if base + j < 2:
                    value = jnp.where(band == 0, 0.0, value)
                if base + j >= 6:
                    value = jnp.where(band == bands - 1, 0.0, value)
                stencil[xx, z, base + j] = value

    for copy in coarse:
        copy.wait_recv()
    zmask = (lax.broadcasted_iota(jnp.int32, (8, 384), 0) // 2) % 2 == 0
    for s in range(2):
        planes = []
        for pair in range(4):
            both = crs[s, pair].astype(F32)
            planes += [both[0:24], both[24:48]]

        def put(at_row, value):
            high = value.astype(BF16)
            low = (value - high.astype(F32)).astype(BF16)
            rows = value.shape[0]
            fields[0, s, at_row : at_row + rows, :] = high
            fields[1, s, at_row : at_row + rows, :] = low

        for d in range(2):
            for xx in range(4):
                pieces = []
                for z in range(2):
                    total = None
                    for j in range(5):
                        c = 2 * z + xx // 2 + j
                        term = stencil[xx, z, c] * planes[c][8 * d : 8 * d + 8]
                        total = term if total is None else total + term
                    pieces.append(total)
                put(d * 64 + xx * 16, jnp.concatenate(pieces, axis=0))
        for pairx in range(2):
            pieces = []
            for xx in (2 * pairx, 2 * pairx + 1):
                total = None
                for c in range(8):
                    w0, w1 = stencil.get((xx, 0, c)), stencil.get((xx, 1, c))
                    if w0 is None and w1 is None:
                        continue
                    w = jnp.where(zmask, 0.0 if w0 is None else w0, 0.0 if w1 is None else w1)
                    term = w * planes[c][16:24]
                    total = term if total is None else total + term
                pieces.append(total)
            put(128 + 16 * pairx, jnp.concatenate(pieces, axis=0))

    own_truth.wait()
    own_climate.wait()
    other_truth.wait_recv()
    xcopies = []
    for ch in range(CHUNKS):
        lo, hi = ch * CHUNK, min((ch + 1) * CHUNK, WIDE)
        width = hi - lo
        w = table[:, lo:hi]
        clim = jnp.dot(pick_c[...], cbuf[:, lo:hi], preferred_element_type=F32)
        sq = an = None
        for s in range(2):
            fine = jnp.dot(fields[0, s], w, preferred_element_type=F32)
            fine += jnp.dot(fields[1, s], w, preferred_element_type=F32)
            actual = jnp.dot(pick[...], tbuf[s, :, lo:hi], preferred_element_type=F32)
            error = fine - actual
            e2 = error * error
            ab = (fine - clim) * (actual - clim)
            sq = e2 if sq is None else sq + e2
            an = ab if an is None else an + ab
        upper = lax.broadcasted_iota(jnp.int32, (8, width), 0) < 4
        for xx in range(4):
            block = slice(16 * xx, 16 * xx + 16)
            block1 = slice(64 + 16 * xx, 64 + 16 * xx + 16)
            tail = slice(128 + 8 * xx, 136 + 8 * xx)
            xsend[xx, ch, 0:16, 0:width] = sq[block] + sq[block1]
            xsend[xx, ch, 16:32, 0:width] = an[block] + an[block1]
            mixed = []
            for t in (sq[tail], an[tail]):
                mixed.append(t + pltpu.roll(t, 4, 0))
            xsend[xx, ch, 32:40, 0:width] = jnp.where(upper, mixed[0], mixed[1])
        for k in range(3):
            xcopies.append(
                send(
                    xsend.at[(x + k + 1) % 4, ch],
                    xrecv.at[k, ch],
                    xssem.at[k, ch],
                    xrsem.at[k, ch],
                    across[k],
                )
            )

    first_half = half == 0
    even = lax.broadcasted_iota(jnp.int32, (8, 256), 0) % 4 < 2
    zcopies = []
    for ch in range(CHUNKS):
        total = xsend[x, ch]
        for k in range(3):
            xcopies[3 * ch + k].wait_recv()
            total += xrecv[k, ch]
        parts = []
        for z in range(2):
            a, b = total[8 * z : 8 * z + 8], total[16 + 8 * z : 24 + 8 * z]
            left, right = total[32:40, 0:256], total[32:40, 256:512]
            if z == 0:
                tail = jnp.where(even, left, pltpu.roll(right, 2, 0))
            else:
                tail = jnp.where(even, pltpu.roll(left, 6, 0), right)
            parts.append(
                jnp.concatenate([a[:, 0:256], b[:, 0:256], a[:, 256:512], b[:, 256:512], tail], axis=0)
            )
        zsend[ch] = jnp.where(first_half, parts[1], parts[0])
        zown[ch] = jnp.where(first_half, parts[0], parts[1])
        zcopies.append(send(zsend.at[ch], zrecv.at[ch], zssem.at[ch], zrsem.at[ch], far))

    for ch in range(CHUNKS):
        zcopies[ch].wait_recv()
        total = (zown[ch] + zrecv[ch]) * (1.0 / 32.0)
        for side in range(2):
            lo = ch * CHUNK + side * 256
            hi = min(lo + 256, WIDE)
            width = hi - lo
            for which in range(2):
                r = 16 * side + 8 * which
                out[which, 0:8, lo:hi] = total[r : r + 8, 0:width]
                r = 32 + 4 * which + 2 * side
                out[which, 8:10, lo:hi] = total[r : r + 2, 0:width]

    for copy in coarse + [other_truth] + xcopies + zcopies:
        copy.wait_send()


def shards(model, truth, climate, starts, lat_w, lon_first, lon_w):
    vmem = pl.BlockSpec(memory_space=pltpu.VMEM)
    smem = pl.BlockSpec(memory_space=pltpu.SMEM)
    hbm = pl.BlockSpec(memory_space=pl.ANY)
    maps = pl.pallas_call(
        kernel,
        out_shape=jax.ShapeDtypeStruct((2, 10, WIDE), F32),
        in_specs=[vmem, hbm, hbm, smem, smem, vmem, vmem],
        out_specs=vmem,
        scratch_shapes=[
            pltpu.VMEM((2, 320, WIDE), BF16),
            pltpu.VMEM((160, WIDE), BF16),
            pltpu.VMEM((2, 4, 48, 384), BF16),
            pltpu.VMEM((2, 2, 160, 384), BF16),
            pltpu.VMEM((384, WIDE), BF16),
            pltpu.VMEM((160, 320), BF16),
            pltpu.VMEM((160, 160), BF16),
            pltpu.VMEM((4, CHUNKS, 40, CHUNK), F32),
            pltpu.VMEM((3, CHUNKS, 40, CHUNK), F32),
            pltpu.VMEM((CHUNKS, 40, 256), F32),
            pltpu.VMEM((CHUNKS, 40, 256), F32),
            pltpu.VMEM((CHUNKS, 40, 256), F32),
            pltpu.SemaphoreType.DMA((2,)),
            pltpu.SemaphoreType.DMA((2,)),
            pltpu.SemaphoreType.DMA((5,)),
            pltpu.SemaphoreType.DMA((5,)),
            pltpu.SemaphoreType.DMA((3, CHUNKS)),
            pltpu.SemaphoreType.DMA((3, CHUNKS)),
            pltpu.SemaphoreType.DMA((CHUNKS,)),
            pltpu.SemaphoreType.DMA((CHUNKS,)),
        ],
        compiler_params=pltpu.CompilerParams(
            collective_id=0, has_side_effects=True, vmem_limit_bytes=40 * 2**20
        ),
    )(
        model.reshape(20, 4, COARSE),
        truth.reshape(320, WIDE),
        climate.reshape(160, WIDE),
        starts,
        lat_w.T,
        lon_first.reshape(1, WIDE),
        lon_w,
    )
    return maps[0].reshape(2, 5, 1, WIDE), maps[1].reshape(2, 5, 1, WIDE)


def solution(mesh):
    in_specs = (
        P("date", None, None, "band", None),
        P("date", None, None, "band", None),
        P(None, None, "band", None),
        P("band"),
        P("band", None),
        P(),
        P(),
    )
    out_specs = (P(None, None, ("band", "date"), None), P(None, None, ("band", "date"), None))
    return jax.shard_map(shards, mesh=mesh, in_specs=in_specs, out_specs=out_specs, check_vma=False)
```

time: 178 us -> 53.4 us (0.30)
  waiting for transfers between devices: 143 us -> 0 us
  Pallas kernels: 0 us -> 47.2 us
  between operations: 14.1 us -> 0.69 us
  starting transfers between devices: 5.36 us -> 0 us
  matrix products: 4.49 us -> 0 us
  other arithmetic: 4.35 us -> 0 us
    reduce_scatter x1 -> x0, waiting for transfers between devices: 143 us -> none  [shards(): lax.psum_scatter(partial_maps, 'date', scatter_dimension=0, tiled=True)]
    pallas_call x0 -> x1, Pallas kernels: none -> 47.2 us  [shards(): pl.pallas_call(kernel, out_shape=jax.ShapeDtypeStruct((2, 10, WIDE), F32)...]
    ppermute x2 -> x0, starting transfers between devices: 5.32 us -> none  [the longest x1 4.03 us: padded(): lax.ppermute(lax.slice_in_dim(block, block.shape[dim] - width, None, axis...]
    dot_general x2 -> x0, matrix products: 4.49 us -> none  [the longest x1 2.27 us: shards(): jnp.dot(flattened_arrays, table, preferred_element_type=jnp.float32)]
    transpose x1 -> x0, local copies, waits for them, and re-layouts: 2.88 us -> none  [shards(): partial_maps = jnp.moveaxis(terms, 3, 0)]
    convert_element_type x2 -> x0, other arithmetic: 1.84 us -> none  [the longest x1 1.13 us: shards(): climate_all = expected_normal.astype(jnp.float32)]
  transfers between devices with their start and end apart: 3 -> 0, of which waited for: 1 -> 0; matrix products, arithmetic and copies ran while one was open for 2% -> 0% of each run, Pallas kernels for 0% -> 0%
where the time goes in v1:
time: 53.4 us; the launch traced here: 53.1 us
  Pallas kernels  47.2 us (88%)
  local copies, waits for them, and re-layouts  5.2 us (10%)
  between operations  0.69 us (1%)
    pallas_call x1, Pallas kernels, shards(): pl.pallas_call(kernel, out_shape=jax.ShapeDtypeStruct((2, 10, WIDE), F32)...  47.2 us
    unnamed x12, local copies, waits for them, and re-layouts  3.07 us
    another operation x2, local copies, waits for them, and re-layouts, shards(): return (maps[0].reshape(2, 5, 1, WIDE), maps[1].reshape(2, 5, 1, WIDE))  1.4 us

profile of v1, /device:TPU:1, one launch (start us, length us, event | category | flops | bytes accessed | tf_op | source)
XLA Modules:
  0.0 53.1 jit_solution(12969999171680438578)
XLA Ops:
  0.6 0.0 copy-start.3
  0.6 0.0 copy-start.4
  0.7 0.0 copy-start.5
  0.7 0.7 %reshape.19.lon_first = s32[1,1440]{1,0:T(1,128)S(1)} reshape(s32[1440]{0:T(1024)} %param.12) | data formatting | bytes 11520 | tf_op jit(solution)/shard_map/reshape | solution.py:285
  1.4 0.0 copy-done.3
  1.4 0.0 copy-done.4
  1.4 0.0 copy-done.5
  1.4 0.0 copy-start
  1.4 1.2 %copy-done = bf16[2,2,5,16,1440]{4,3,2,1,0:T(8,128)(2,1)S(1)} copy-done((bf16[2,2,5,16,1440]{4,3,2,1,0:T(8,128)(2,1)S(1)}, bf16[2,2,5,16,1440]{4,3,2,1,0:T(8,128)(2,1)}, u32[]{:S(2)}) %copy-start) | copy-done | bytes 921624
  2.6 0.0 copy-start.1
  2.6 1.0 %copy-done.1 = bf16[2,5,16,1440]{3,2,1,0:T(8,128)(2,1)S(1)} copy-done((bf16[2,5,16,1440]{3,2,1,0:T(8,128)(2,1)S(1)}, bf16[2,5,16,1440]{3,2,1,0:T(8,128)(2,1)}, u32[]{:S(2)}) %copy-start.1) | copy-done | bytes 460824
  3.6 0.0 copy-start.2
  3.6 0.8 %copy-done.2 = bf16[2,2,5,4,360]{4,3,2,1,0:T(4,128)(2,1)S(1)} copy-done((bf16[2,2,5,4,360]{4,3,2,1,0:T(4,128)(2,1)S(1)}, bf16[2,2,5,4,360]{4,3,2,1,0:T(4,128)(2,1)}, u32[]{:S(2)}) %copy-start.2) | copy-done | bytes 57624
  4.5 47.2 %shard_map.86 = f32[2,10,1440]{2,1,0:T(8,128)S(1)} custom-call(bf16[20,4,360]{2,1,0:T(4,128)(2,1)S(1)} %bitcast.6, bf16[320,1440]{1,0:T(8,128)(2,1)S(1)} %bitcast.4, bf16[160,1440]{1,0:T(8,128)(2,1)S(1)} %bitcast.5, s32[16]{0:T(128)S(1)} %copy-done.5, f32[4,16]{1,0:T(4,128)S(1)} %bitcast.7, s32[1,1440]{1,0:T(1,128)S(1)} %reshape.19.lon_first, ...), custom_call_target="tpu_custom_call" | custom-call | tf_op jit(solution)/shard_map/pallas_call | solution.py:249
  51.7 0.7 %reshape_squeeze.7 = f32[2,5,1,1440]{3,2,1,0:T(1,128)} reshape(f32[1,10,1440]{2,1,0:T(8,128)S(1)} %get-tuple-element.4) | data formatting | bytes 115200 | tf_op jit(solution)/shard_map/reshape;squeeze | solution.py:288
  52.4 0.7 %reshape_squeeze.6 = f32[2,5,1,1440]{3,2,1,0:T(1,128)} reshape(f32[1,10,1440]{2,1,0:T(8,128)S(1)} %get-tuple-element.5) | data formatting | bytes 115200 | tf_op jit(solution)/shard_map/reshape;squeeze | solution.py:288
  (1 shorter events, 0.0 us)
Async XLA Ops:
  0.6 0.8 %copy-start.3 = (bf16[4,1440]{1,0:T(4,128)(2,1)S(1)}, bf16[4,1440]{1,0:T(4,128)(2,1)}, u32[]{:S(2)}) copy-start(bf16[4,1440]{1,0:T(4,128)(2,1)} %lon_w.1) | copy-start | bytes 34564
  0.6 0.7 %copy-start.4 = (f32[16,4]{0,1:T(4,128)S(1)}, f32[16,4]{0,1:T(4,128)}, u32[]{:S(2)}) copy-start(f32[16,4]{0,1:T(4,128)} %param.11) | copy-start | bytes 772
  0.7 0.7 %copy-start.5 = (s32[16]{0:T(128)S(1)}, s32[16]{0:T(128)}, u32[]{:S(2)}) copy-start(s32[16]{0:T(128)} %starts.1) | copy-start | bytes 196
  1.4 1.2 %copy-start = (bf16[2,2,5,16,1440]{4,3,2,1,0:T(8,128)(2,1)S(1)}, bf16[2,2,5,16,1440]{4,3,2,1,0:T(8,128)(2,1)}, u32[]{:S(2)}) copy-start(bf16[2,2,5,16,1440]{4,3,2,1,0:T(8,128)(2,1)} %param.8) | copy-start | bytes 2764804
  2.6 1.0 %copy-start.1 = (bf16[2,5,16,1440]{3,2,1,0:T(8,128)(2,1)S(1)}, bf16[2,5,16,1440]{3,2,1,0:T(8,128)(2,1)}, u32[]{:S(2)}) copy-start(bf16[2,5,16,1440]{3,2,1,0:T(8,128)(2,1)} %param.9) | copy-start | bytes 1382404
  3.6 0.8 %copy-start.2 = (bf16[2,2,5,4,360]{4,3,2,1,0:T(4,128)(2,1)S(1)}, bf16[2,2,5,4,360]{4,3,2,1,0:T(4,128)(2,1)}, u32[]{:S(2)}) copy-start(bf16[2,2,5,4,360]{4,3,2,1,0:T(4,128)(2,1)} %param.7) | copy-start | bytes 172804

commit v2 on v1

--- a/solution.py
+++ b/solution.py
@@ -16,11 +16,53 @@
 CHUNKS = 3
 
 
+def upper_rows():
+    return lax.broadcasted_iota(jnp.int32, (8, 128), 0) < 4
+
+
+def encode(sqs, ans, tails):
+    upper = upper_rows()
+
+    def scale(tiles, keep):
+        most = functools.reduce(jnp.maximum, [jnp.abs(t) for t in tiles])
+        more = functools.reduce(jnp.maximum, [jnp.abs(t) for t in tails])
+        most = jnp.maximum(jnp.maximum(most, jnp.where(keep, more, 0.0)), 1e-25)
+        return jnp.ceil(jnp.log(most) * (8.0 / 0.6931471805599453) + 0.01)
+
+    e_sq, e_an = scale(sqs, upper), scale(ans, jnp.logical_not(upper))
+    up_sq, up_an = (32767.0 * jnp.exp2(e * -0.125) for e in (e_sq, e_an))
+    up_tail = jnp.where(upper, up_sq, up_an)
+    words = []
+    for tiles, up in ((sqs, up_sq), (ans, up_an), (tails, up_tail)):
+        codes = [jnp.round(t * up).astype(jnp.int32) for t in tiles]
+        for low, high in zip(codes[0::2], codes[1::2], strict=True):
+            words.append((high << 16) | (low & 0xFFFF))
+    words.append((e_sq.astype(jnp.int32) << 16) | (e_an.astype(jnp.int32) & 0xFFFF))
+    return jnp.concatenate(words, axis=0)
+
+
+def decode(words, n, n_tail):
+    count = words.shape[0] // 8
+    tiles = [words[8 * i : 8 * i + 8] for i in range(count)]
+
+    def both(t):
+        return ((t << 16) >> 16).astype(F32), (t >> 16).astype(F32)
+
+    e_an, e_sq = both(tiles[-1])
+    down_sq, down_an = (jnp.exp2(e * 0.125) * (1.0 / 32767.0) for e in (e_sq, e_an))
+    down_tail = jnp.where(upper_rows(), down_sq, down_an)
+    values = []
+    for i, t in enumerate(tiles[:-1]):
+        down = down_sq if i < n // 2 else down_an if i < n else down_tail
+        values += [v * down for v in both(t)]
+    return values[:n], values[n : 2 * n], values[2 * n :]
+
+
 def kernel(
     model, truth, climate, starts, lat_w, lon_first, lon_w,
     out,
-    tbuf, cbuf, crs, fields, table, pick, pick_c, xsend, xrecv, zsend, zown, zrecv,
-    lsem, tsem, csend, crecv, xssem, xrsem, zssem, zrsem,
+    mbuf, tbuf, cbuf, crs, fields, table, pick, pick_c, parts, xsend, xrecv, zsend, zown, zrecv,
+    lsem, tsem, csend, crecv, xssem, xrsem, zssem, zrsem, far_in,
 ):
     date = lax.axis_index("date")
     band = lax.axis_index("band")
@@ -35,19 +77,30 @@
     sibling = (at(half, x, 1 - core), band)
     across = [(at(half, (x + k) % 4, core), band) for k in (1, 2, 3)]
     far = (at(1 - half, x, core), band)
-    up, down = (band + 1) % bands, (band + bands - 1) % bands
+    up, down = band + 1, band - 1
     near = [(date, up), (date, down), (at(half, x, 1 - core), up), (at(half, x, 1 - core), down)]
+    not_last, not_first = band < bands - 1, band > 0
     barrier = pltpu.get_barrier_semaphore()
-    for partner in [far, sibling] + near + across:
+
+    def greet(partner):
         pl.semaphore_signal(barrier, inc=1, device_id=partner, device_id_type=MESH)
 
+    pl.when(half == 0)(lambda: greet(far))
+    pl.when(not_last)(lambda: [greet(near[0]), greet(near[2])] and None)
+    pl.when(not_first)(lambda: [greet(near[1]), greet(near[3])] and None)
+    for partner in [sibling] + across:
+        greet(partner)
+
+    own_model = pltpu.make_async_copy(model, mbuf, lsem.at[2])
+    own_model.start()
     own_truth = pltpu.make_async_copy(truth, tbuf.at[0], lsem.at[0])
     own_truth.start()
     own_climate = pltpu.make_async_copy(climate, cbuf, lsem.at[1])
     own_climate.start()
 
     crs[0, 1:3] = jnp.zeros((2, 48, 384), BF16)
-    m = model[...].astype(F32)
+    own_model.wait()
+    m = mbuf[...].astype(F32)
     for pair in range(2):
         rows = []
         for k in (2 * pair, 2 * pair + 1):
@@ -56,26 +109,50 @@
             a, b = plane[8:10], plane[18:20]
             rows += [a, a, b, b]
         crs[0, 1 + pair, :, 0:COARSE] = jnp.concatenate(rows, axis=0).astype(BF16)
-
-    pl.semaphore_wait(barrier, 9)
-
-    def send(src, dst, ssem, rsem, device):
-        copy = pltpu.make_async_remote_copy(
+    pl.semaphore_wait(
+        barrier,
+        4 + half + 2 * jnp.where(not_last, 1, 0) + 2 * jnp.where(not_first, 1, 0),
+    )
+
+    pending = []
+
+    def make(src, dst, ssem, rsem, device):
+        return pltpu.make_async_remote_copy(
             src_ref=src, dst_ref=dst, send_sem=ssem, recv_sem=rsem, device_id=device, device_id_type=MESH
         )
+
+    def send(*what):
+        copy = make(*what)
         copy.start()
+        pending.append(copy)
         return copy
 
-    coarse = [
-        send(crs.at[0, 2], crs.at[0, 0], csend.at[0], crecv.at[0], near[0]),
-        send(crs.at[0, 1], crs.at[0, 3], csend.at[1], crecv.at[1], near[1]),
-        send(crs.at[0, 2], crs.at[1, 0], csend.at[2], crecv.at[2], near[2]),
-        send(crs.at[0, 1], crs.at[1, 3], csend.at[3], crecv.at[3], near[3]),
-        send(crs.at[0, pl.ds(1, 2)], crs.at[1, pl.ds(1, 2)], csend.at[4], crecv.at[4], sibling),
+    edges = [
+        make(crs.at[0, 2], crs.at[0, 0], csend.at[0], crecv.at[0], near[0]),
+        make(crs.at[0, 1], crs.at[0, 3], csend.at[1], crecv.at[1], near[1]),
+        make(crs.at[0, 2], crs.at[1, 0], csend.at[2], crecv.at[2], near[2]),
+        make(crs.at[0, 1], crs.at[1, 3], csend.at[3], crecv.at[3], near[3]),
     ]
+
+    @pl.when(not_last)
+    def _():
+        edges[0].start()
+        edges[2].start()
+
+    @pl.when(not_first)
+    def _():
+        edges[1].start()
+        edges[3].start()
+
+    swap = send(crs.at[0, pl.ds(1, 2)], crs.at[1, pl.ds(1, 2)], csend.at[4], crecv.at[4], sibling)
+
+    @pl.when(half == 1)
+    def _():
+        pl.semaphore_signal(far_in, inc=1, device_id=far, device_id_type=MESH)
+
     other_truth = send(truth, tbuf.at[1], tsem.at[0], tsem.at[1], sibling)
 
-    first_all = lon_first[...]
+    first_all = lon_first[...].reshape(1, WIDE)
     weights_all = lon_w[...].astype(F32)
     for start in range(0, WIDE, CHUNK):
         width = min(CHUNK, WIDE - start)
@@ -100,7 +177,7 @@
     pick_c[...] = (column == target).astype(F32).astype(BF16)
     column = lax.broadcasted_iota(jnp.int32, (160, 320), 1)
     pick[...] = (column == d_of * 160 + target).astype(F32).astype(BF16)
-    xsend[:, CHUNKS - 1, :, 384:512] = jnp.zeros((4, 40, 128), F32)
+    parts[:, CHUNKS - 1, :, 384:512] = jnp.zeros((4, 40, 128), F32)
 
     stencil = {}
     for xx in range(4):
@@ -113,15 +190,27 @@
             five += [jnp.where(late == 0, w[j], w[j - 1]) for j in (1, 2, 3)]
             five += [jnp.where(late == 0, 0.0, w[3])]
             for j in range(5):
-                value = five[j]
-                if base + j < 2:
-                    value = jnp.where(band == 0, 0.0, value)
-                if base + j >= 6:
-                    value = jnp.where(band == bands - 1, 0.0, value)
-                stencil[xx, z, base + j] = value
-
-    for copy in coarse:
-        copy.wait_recv()
+                stencil[xx, z, base + j] = five[j]
+
+    @pl.when(not_first)
+    def _():
+        edges[0].wait_recv()
+        edges[2].wait_recv()
+
+    @pl.when(not_last)
+    def _():
+        edges[1].wait_recv()
+        edges[3].wait_recv()
+
+    @pl.when(band == 0)
+    def _():
+        crs[:, 0] = jnp.zeros((2, 48, 384), BF16)
+
+    @pl.when(band == bands - 1)
+    def _():
+        crs[:, 3] = jnp.zeros((2, 48, 384), BF16)
+
+    swap.wait_recv()
     zmask = (lax.broadcasted_iota(jnp.int32, (8, 384), 0) // 2) % 2 == 0
     for s in range(2):
         planes = []
@@ -185,12 +274,19 @@
             block = slice(16 * xx, 16 * xx + 16)
             block1 = slice(64 + 16 * xx, 64 + 16 * xx + 16)
             tail = slice(128 + 8 * xx, 136 + 8 * xx)
-            xsend[xx, ch, 0:16, 0:width] = sq[block] + sq[block1]
-            xsend[xx, ch, 16:32, 0:width] = an[block] + an[block1]
+            parts[xx, ch, 0:16, 0:width] = sq[block] + sq[block1]
+            parts[xx, ch, 16:32, 0:width] = an[block] + an[block1]
             mixed = []
             for t in (sq[tail], an[tail]):
                 mixed.append(t + pltpu.roll(t, 4, 0))
-            xsend[xx, ch, 32:40, 0:width] = jnp.where(upper, mixed[0], mixed[1])
+            parts[xx, ch, 32:40, 0:width] = jnp.where(upper, mixed[0], mixed[1])
+            block = parts[xx, ch]
+            tiles = [block[:, 128 * j : 128 * j + 128] for j in range(4)]
+            xsend[xx, ch] = encode(
+                [t[r : r + 8] for r in (0, 8) for t in tiles],
+                [t[r : r + 8] for r in (16, 24) for t in tiles],
+                [t[32:40] for t in tiles],
+            )
         for k in range(3):
             xcopies.append(
                 send(
@@ -206,11 +302,14 @@
     even = lax.broadcasted_iota(jnp.int32, (8, 256), 0) % 4 < 2
     zcopies = []
     for ch in range(CHUNKS):
-        total = xsend[x, ch]
         for k in range(3):
             xcopies[3 * ch + k].wait_recv()
-            total += xrecv[k, ch]
-        parts = []
+        total = parts[x, ch]
+        for k in range(3):
+            sqs, ans, tails = decode(xrecv[k, ch], 8, 4)
+            rows = [jnp.concatenate(g, axis=1) for g in (sqs[0:4], sqs[4:8], ans[0:4], ans[4:8], tails)]
+            total += jnp.concatenate(rows, axis=0)
+        kept = []
         for z in range(2):
             a, b = total[8 * z : 8 * z + 8], total[16 + 8 * z : 24 + 8 * z]
             left, right = total[32:40, 0:256], total[32:40, 256:512]
@@ -218,28 +317,47 @@
                 tail = jnp.where(even, left, pltpu.roll(right, 2, 0))
             else:
                 tail = jnp.where(even, pltpu.roll(left, 6, 0), right)
-            parts.append(
+            kept.append(
                 jnp.concatenate([a[:, 0:256], b[:, 0:256], a[:, 256:512], b[:, 256:512], tail], axis=0)
             )
-        zsend[ch] = jnp.where(first_half, parts[1], parts[0])
-        zown[ch] = jnp.where(first_half, parts[0], parts[1])
+        going = jnp.where(first_half, kept[1], kept[0])
+        zown[ch] = jnp.where(first_half, kept[0], kept[1])
+        tiles = [going[:, 128 * j : 128 * j + 128] for j in range(2)]
+        zsend[ch] = encode(
+            [t[r : r + 8] for r in (0, 16) for t in tiles],
+            [t[r : r + 8] for r in (8, 24) for t in tiles],
+            [t[32:40] for t in tiles],
+        )
+        if ch == 0:
+            pl.when(first_half)(lambda: pl.semaphore_wait(far_in, 1))
         zcopies.append(send(zsend.at[ch], zrecv.at[ch], zssem.at[ch], zrsem.at[ch], far))
 
     for ch in range(CHUNKS):
         zcopies[ch].wait_recv()
-        total = (zown[ch] + zrecv[ch]) * (1.0 / 32.0)
+        sqs, ans, tails = decode(zrecv[ch], 4, 2)
+        rows = [jnp.concatenate(g, axis=1) for g in (sqs[0:2], ans[0:2], sqs[2:4], ans[2:4], tails)]
+        total = (zown[ch] + jnp.concatenate(rows, axis=0)) * (1.0 / 32.0)
         for side in range(2):
             lo = ch * CHUNK + side * 256
             hi = min(lo + 256, WIDE)
             width = hi - lo
             for which in range(2):
                 r = 16 * side + 8 * which
-                out[which, 0:8, lo:hi] = total[r : r + 8, 0:width]
+                out[which, 0:8, 0, lo:hi] = total[r : r + 8, 0:width]
                 r = 32 + 4 * which + 2 * side
-                out[which, 8:10, lo:hi] = total[r : r + 2, 0:width]
-
-    for copy in coarse + [other_truth] + xcopies + zcopies:
+                out[which, 8:10, 0, lo:hi] = total[r : r + 2, 0:width]
+    for copy in pending:
         copy.wait_send()
+
+    @pl.when(not_last)
+    def _():
+        edges[0].wait_send()
+        edges[2].wait_send()
+
+    @pl.when(not_first)
+    def _():
+        edges[1].wait_send()
+        edges[3].wait_send()
 
 
 def shards(model, truth, climate, starts, lat_w, lon_first, lon_w):
@@ -248,10 +366,11 @@
     hbm = pl.BlockSpec(memory_space=pl.ANY)
     maps = pl.pallas_call(
         kernel,
-        out_shape=jax.ShapeDtypeStruct((2, 10, WIDE), F32),
-        in_specs=[vmem, hbm, hbm, smem, smem, vmem, vmem],
+        out_shape=jax.ShapeDtypeStruct((2, 10, 1, WIDE), F32),
+        in_specs=[hbm, hbm, hbm, smem, smem, vmem, vmem],
         out_specs=vmem,
         scratch_shapes=[
+            pltpu.VMEM((20, 4, COARSE), BF16),
             pltpu.VMEM((2, 320, WIDE), BF16),
             pltpu.VMEM((160, WIDE), BF16),
             pltpu.VMEM((2, 4, 48, 384), BF16),
@@ -260,11 +379,12 @@
             pltpu.VMEM((160, 320), BF16),
             pltpu.VMEM((160, 160), BF16),
             pltpu.VMEM((4, CHUNKS, 40, CHUNK), F32),
-            pltpu.VMEM((3, CHUNKS, 40, CHUNK), F32),
+            pltpu.VMEM((4, CHUNKS, 88, 128), jnp.int32),
+            pltpu.VMEM((3, CHUNKS, 88, 128), jnp.int32),
+            pltpu.VMEM((CHUNKS, 48, 128), jnp.int32),
             pltpu.VMEM((CHUNKS, 40, 256), F32),
-            pltpu.VMEM((CHUNKS, 40, 256), F32),
-            pltpu.VMEM((CHUNKS, 40, 256), F32),
-            pltpu.SemaphoreType.DMA((2,)),
+            pltpu.VMEM((CHUNKS, 48, 128), jnp.int32),
+            pltpu.SemaphoreType.DMA((3,)),
             pltpu.SemaphoreType.DMA((2,)),
             pltpu.SemaphoreType.DMA((5,)),
             pltpu.SemaphoreType.DMA((5,)),
@@ -272,9 +392,10 @@
             pltpu.SemaphoreType.DMA((3, CHUNKS)),
             pltpu.SemaphoreType.DMA((CHUNKS,)),
             pltpu.SemaphoreType.DMA((CHUNKS,)),
+            pltpu.SemaphoreType.REGULAR,
         ],
         compiler_params=pltpu.CompilerParams(
-            collective_id=0, has_side_effects=True, vmem_limit_bytes=40 * 2**20
+            collective_id=0, has_side_effects=True, vmem_limit_bytes=60 * 2**20
         ),
     )(
         model.reshape(20, 4, COARSE),
@@ -282,7 +403,7 @@
         climate.reshape(160, WIDE),
         starts,
         lat_w.T,
-        lon_first.reshape(1, WIDE),
+        lon_first,
         lon_w,
     )
     return maps[0].reshape(2, 5, 1, WIDE), maps[1].reshape(2, 5, 1, WIDE)

time: 53.4 us -> 40.1 us (0.75)
  Pallas kernels: 47.2 us -> 37.5 us
  local copies, waits for them, and re-layouts: 5.2 us -> 1.52 us
    pallas_call x1, Pallas kernels: 47.2 us -> 37.5 us  [shards(): pl.pallas_call(kernel, out_shape=jax.ShapeDtypeStruct((2, 10, 1, WIDE), F...]
    unnamed x12 -> x0, local copies, waits for them, and re-layouts: 3.07 us -> none
    slice x1, local copies, waits for them, and re-layouts: 0.02 us -> 1.52 us  [shards(): return (maps[0].reshape(2, 5, 1, WIDE), maps[1].reshape(2, 5, 1, WIDE))]
    another operation x2 -> x0, local copies, waits for them, and re-layouts: 1.4 us -> none  [shards(): return (maps[0].reshape(2, 5, 1, WIDE), maps[1].reshape(2, 5, 1, WIDE))]
    reshape x1 -> x0, local copies, waits for them, and re-layouts: 0.72 us -> none  [shards(): lon_first.reshape(1, WIDE)]
where the time goes in v2:
time: 40.1 us; the launch traced here: 39.7 us
  Pallas kernels  37.5 us (94%)
  local copies, waits for them, and re-layouts  1.52 us (4%)
  between operations  0.64 us (2%)
    pallas_call x1, Pallas kernels, shards(): pl.pallas_call(kernel, out_shape=jax.ShapeDtypeStruct((2, 10, 1, WIDE), F...  37.5 us
    slice x1, local copies, waits for them, and re-layouts, shards(): return (maps[0].reshape(2, 5, 1, WIDE), maps[1].reshape(2, 5, 1, WIDE))  1.52 us

profile of v2, /device:TPU:1, one launch (start us, length us, event | category | flops | bytes accessed | tf_op | source)
XLA Modules:
  0.0 39.7 jit_solution(14698987908899916665)
XLA Ops:
  0.6 37.5 %shard_map.86 = f32[2,10,1,1440]{3,2,1,0:T(1,128)} custom-call(bf16[20,4,360]{2,1,0:T(4,128)(2,1)} %bitcast.8, bf16[320,1440]{1,0:T(8,128)(2,1)} %bitcast.6, bf16[160,1440]{1,0:T(8,128)(2,1)} %bitcast.7, s32[16]{0:T(128)} %starts.1, f32[4,16]{1,0:T(4,128)} %bitcast.11, s32[1440]{0:T(1024)} %lon_first.1, bf16[4,1440]{1,0:T(4,128)(2,1)} %lon_w.1), custom_call_target="tpu_custom_call" | custom-call | tf_op jit(solution)/shard_map/pallas_call | solution.py:367
  38.2 1.5 %fusion = (f32[1,10,1,1440]{3,2,1,0:T(1,128)}, f32[1,10,1,1440]{3,2,1,0:T(1,128)}) fusion(f32[2,10,1,1440]{3,2,1,0:T(1,128)} %shard_map.86), kind=kLoop, calls=%fused_computation | loop fusion | bytes 230400 | tf_op jit(solution)/shard_map/slice | solution.py:409

commit v3 on v2

--- a/solution.py
+++ b/solution.py
@@ -59,9 +59,9 @@
 
 
 def kernel(
-    model, truth, climate, starts, lat_w, lon_first, lon_w,
+    model, truth, climate, starts_in, lat_w_in, lon_first_in, lon_w_in,
     out,
-    mbuf, tbuf, cbuf, crs, fields, table, pick, pick_c, parts, xsend, xrecv, zsend, zown, zrecv,
+    starts, lat_w, lon_first, lon_w, mbuf, tbuf, cbuf, crs, fields, table, pick, pick_c, actual, anomaly, mixed, parts, xsend, xrecv, zsend, zown, zrecv,
     lsem, tsem, csend, crecv, xssem, xrsem, zssem, zrsem, far_in,
 ):
     date = lax.axis_index("date")
@@ -97,6 +97,14 @@
     own_truth.start()
     own_climate = pltpu.make_async_copy(climate, cbuf, lsem.at[1])
     own_climate.start()
+    small = [
+        pltpu.make_async_copy(source, target, lsem.at[3 + i])
+        for i, (source, target) in enumerate(
+            [(starts_in, starts), (lat_w_in, lat_w), (lon_first_in, lon_first), (lon_w_in, lon_w)]
+        )
+    ]
+    for copy in small:
+        copy.start()
 
     crs[0, 1:3] = jnp.zeros((2, 48, 384), BF16)
     own_model.wait()
@@ -152,6 +160,8 @@
 
     other_truth = send(truth, tbuf.at[1], tsem.at[0], tsem.at[1], sibling)
 
+    for copy in small:
+        copy.wait()
     first_all = lon_first[...].reshape(1, WIDE)
     weights_all = lon_w[...].astype(F32)
     for start in range(0, WIDE, CHUNK):
@@ -177,7 +187,8 @@
     pick_c[...] = (column == target).astype(F32).astype(BF16)
     column = lax.broadcasted_iota(jnp.int32, (160, 320), 1)
     pick[...] = (column == d_of * 160 + target).astype(F32).astype(BF16)
-    parts[:, CHUNKS - 1, :, 384:512] = jnp.zeros((4, 40, 128), F32)
+    mixed[CHUNKS - 1, :, :, 384:512] = jnp.zeros((4, 8, 128), F32)
+    parts[:, :, CHUNKS - 1, 16:32, 128:256] = jnp.zeros((4, 2, 16, 128), F32)
 
     stencil = {}
     for xx in range(4):
@@ -191,6 +202,18 @@
             five += [jnp.where(late == 0, 0.0, w[3])]
             for j in range(5):
                 stencil[xx, z, base + j] = five[j]
+
+    spans = [(lo, min(lo + CHUNK, WIDE)) for lo in range(0, WIDE, CHUNK)]
+    own_climate.wait()
+    own_truth.wait()
+    for s in range(2):
+        if s == 1:
+            other_truth.wait_recv()
+        for lo, hi in spans:
+            t = jnp.dot(pick[...], tbuf[s, :, lo:hi], preferred_element_type=F32)
+            clim = jnp.dot(pick_c[...], cbuf[:, lo:hi], preferred_element_type=F32)
+            actual[s, :, lo:hi] = t
+            anomaly[s, :, lo:hi] = t - clim
 
     @pl.when(not_first)
     def _():
@@ -250,95 +273,91 @@
                 pieces.append(total)
             put(128 + 16 * pairx, jnp.concatenate(pieces, axis=0))
 
-    own_truth.wait()
-    own_climate.wait()
-    other_truth.wait_recv()
-    xcopies = []
-    for ch in range(CHUNKS):
-        lo, hi = ch * CHUNK, min((ch + 1) * CHUNK, WIDE)
+    going, staying = 1 - half, half
+    even = lax.broadcasted_iota(jnp.int32, (8, 256), 0) % 4 < 2
+
+    def coded(block):
+        tiles = [block[:, 0:128], block[:, 128:256]]
+        return encode(
+            [t[r : r + 8] for r in (0, 16) for t in tiles],
+            [t[r : r + 8] for r in (8, 24) for t in tiles],
+            [t[32:40] for t in tiles],
+        )
+
+    def plain(words):
+        sqs, ans, tails = decode(words, 4, 2)
+        rows = [jnp.concatenate(g, axis=1) for g in (sqs[0:2], ans[0:2], sqs[2:4], ans[2:4], tails)]
+        return jnp.concatenate(rows, axis=0)
+
+    def hand_over(which, rows, ch):
+        copies = []
+        for k in range(3):
+            xsend[k, which, ch] = coded(parts[(x + k + 1) % 4, rows, ch])
+            copies.append(
+                send(
+                    xsend.at[k, which, ch],
+                    xrecv.at[k, which, ch],
+                    xssem.at[k, which, ch],
+                    xrsem.at[k, which, ch],
+                    across[k],
+                )
+            )
+        return copies
+
+    def collect(which, rows, ch, copies):
+        total = parts[x, rows, ch]
+        for k in range(3):
+            copies[k].wait_recv()
+            total += plain(xrecv[k, which, ch])
+        return total
+
+    first, second = [], []
+    for ch, (lo, hi) in enumerate(spans):
         width = hi - lo
         w = table[:, lo:hi]
-        clim = jnp.dot(pick_c[...], cbuf[:, lo:hi], preferred_element_type=F32)
         sq = an = None
         for s in range(2):
             fine = jnp.dot(fields[0, s], w, preferred_element_type=F32)
             fine += jnp.dot(fields[1, s], w, preferred_element_type=F32)
-            actual = jnp.dot(pick[...], tbuf[s, :, lo:hi], preferred_element_type=F32)
-            error = fine - actual
+            error = fine - actual[s, :, lo:hi]
+            true_anomaly = anomaly[s, :, lo:hi]
             e2 = error * error
-            ab = (fine - clim) * (actual - clim)
+            ab = (error + true_anomaly) * true_anomaly
             sq = e2 if sq is None else sq + e2
             an = ab if an is None else an + ab
         upper = lax.broadcasted_iota(jnp.int32, (8, width), 0) < 4
         for xx in range(4):
-            block = slice(16 * xx, 16 * xx + 16)
-            block1 = slice(64 + 16 * xx, 64 + 16 * xx + 16)
             tail = slice(128 + 8 * xx, 136 + 8 * xx)
-            parts[xx, ch, 0:16, 0:width] = sq[block] + sq[block1]
-            parts[xx, ch, 16:32, 0:width] = an[block] + an[block1]
-            mixed = []
-            for t in (sq[tail], an[tail]):
-                mixed.append(t + pltpu.roll(t, 4, 0))
-            parts[xx, ch, 32:40, 0:width] = jnp.where(upper, mixed[0], mixed[1])
-            block = parts[xx, ch]
-            tiles = [block[:, 128 * j : 128 * j + 128] for j in range(4)]
-            xsend[xx, ch] = encode(
-                [t[r : r + 8] for r in (0, 8) for t in tiles],
-                [t[r : r + 8] for r in (16, 24) for t in tiles],
-                [t[32:40] for t in tiles],
-            )
-        for k in range(3):
-            xcopies.append(
-                send(
-                    xsend.at[(x + k + 1) % 4, ch],
-                    xrecv.at[k, ch],
-                    xssem.at[k, ch],
-                    xrsem.at[k, ch],
-                    across[k],
-                )
-            )
-
-    first_half = half == 0
-    even = lax.broadcasted_iota(jnp.int32, (8, 256), 0) % 4 < 2
+            both = [t + pltpu.roll(t, 4, 0) for t in (sq[tail], an[tail])]
+            mixed[ch, xx, :, 0:width] = jnp.where(upper, both[0], both[1])
+            left, right = mixed[ch, xx, :, 0:256], mixed[ch, xx, :, 256:512]
+            parts[xx, 0, ch, 32:40] = jnp.where(even, left, pltpu.roll(right, 2, 0))
+            parts[xx, 1, ch, 32:40] = jnp.where(even, pltpu.roll(left, 6, 0), right)
+            for z in range(2):
+                r = 16 * xx + 8 * z
+                for i, t in enumerate((sq, an)):
+                    value = t[r : r + 8] + t[64 + r : 72 + r]
+                    parts[xx, z, ch, 8 * i : 8 * i + 8] = value[:, 0:256]
+                    parts[xx, z, ch, 16 + 8 * i : 24 + 8 * i, 0 : width - 256] = value[:, 256:width]
+        first.append(hand_over(0, going, ch))
+    for ch in range(CHUNKS):
+        second.append(hand_over(1, staying, ch))
+
     zcopies = []
     for ch in range(CHUNKS):
-        for k in range(3):
-            xcopies[3 * ch + k].wait_recv()
-        total = parts[x, ch]
-        for k in range(3):
-            sqs, ans, tails = decode(xrecv[k, ch], 8, 4)
-            rows = [jnp.concatenate(g, axis=1) for g in (sqs[0:4], sqs[4:8], ans[0:4], ans[4:8], tails)]
-            total += jnp.concatenate(rows, axis=0)
-        kept = []
-        for z in range(2):
-            a, b = total[8 * z : 8 * z + 8], total[16 + 8 * z : 24 + 8 * z]
-            left, right = total[32:40, 0:256], total[32:40, 256:512]
-            if z == 0:
-                tail = jnp.where(even, left, pltpu.roll(right, 2, 0))
-            else:
-                tail = jnp.where(even, pltpu.roll(left, 6, 0), right)
-            kept.append(
-                jnp.concatenate([a[:, 0:256], b[:, 0:256], a[:, 256:512], b[:, 256:512], tail], axis=0)
-            )
-        going = jnp.where(first_half, kept[1], kept[0])
-        zown[ch] = jnp.where(first_half, kept[0], kept[1])
-        tiles = [going[:, 128 * j : 128 * j + 128] for j in range(2)]
-        zsend[ch] = encode(
-            [t[r : r + 8] for r in (0, 16) for t in tiles],
-            [t[r : r + 8] for r in (8, 24) for t in tiles],
-            [t[32:40] for t in tiles],
-        )
+        zsend[ch] = coded(collect(0, going, ch, first[ch]))
         if ch == 0:
-            pl.when(first_half)(lambda: pl.semaphore_wait(far_in, 1))
+            pl.when(half == 0)(lambda: pl.semaphore_wait(far_in, 1))
         zcopies.append(send(zsend.at[ch], zrecv.at[ch], zssem.at[ch], zrsem.at[ch], far))
 
     for ch in range(CHUNKS):
+        zown[ch] = collect(1, staying, ch, second[ch])
+
+    for ch, (start, _) in enumerate(spans):
         zcopies[ch].wait_recv()
-        sqs, ans, tails = decode(zrecv[ch], 4, 2)
-        rows = [jnp.concatenate(g, axis=1) for g in (sqs[0:2], ans[0:2], sqs[2:4], ans[2:4], tails)]
-        total = (zown[ch] + jnp.concatenate(rows, axis=0)) * (1.0 / 32.0)
+        total = (zown[ch] + plain(zrecv[ch])) * (1.0 / 32.0)
         for side in range(2):
-            lo = ch * CHUNK + side * 256
+            lo = start + side * 256
             hi = min(lo + 256, WIDE)
             width = hi - lo
             for which in range(2):
@@ -346,6 +365,7 @@
                 out[which, 0:8, 0, lo:hi] = total[r : r + 8, 0:width]
                 r = 32 + 4 * which + 2 * side
                 out[which, 8:10, 0, lo:hi] = total[r : r + 2, 0:width]
+
     for copy in pending:
         copy.wait_send()
 
@@ -362,14 +382,17 @@
 
 def shards(model, truth, climate, starts, lat_w, lon_first, lon_w):
     vmem = pl.BlockSpec(memory_space=pltpu.VMEM)
-    smem = pl.BlockSpec(memory_space=pltpu.SMEM)
     hbm = pl.BlockSpec(memory_space=pl.ANY)
     maps = pl.pallas_call(
         kernel,
         out_shape=jax.ShapeDtypeStruct((2, 10, 1, WIDE), F32),
-        in_specs=[hbm, hbm, hbm, smem, smem, vmem, vmem],
+        in_specs=[hbm] * 7,
         out_specs=vmem,
         scratch_shapes=[
+            pltpu.SMEM((16,), jnp.int32),
+            pltpu.SMEM((4, 16), F32),
+            pltpu.VMEM((WIDE,), jnp.int32),
+            pltpu.VMEM((4, WIDE), BF16),
             pltpu.VMEM((20, 4, COARSE), BF16),
             pltpu.VMEM((2, 320, WIDE), BF16),
             pltpu.VMEM((160, WIDE), BF16),
@@ -378,33 +401,41 @@
             pltpu.VMEM((384, WIDE), BF16),
             pltpu.VMEM((160, 320), BF16),
             pltpu.VMEM((160, 160), BF16),
-            pltpu.VMEM((4, CHUNKS, 40, CHUNK), F32),
-            pltpu.VMEM((4, CHUNKS, 88, 128), jnp.int32),
-            pltpu.VMEM((3, CHUNKS, 88, 128), jnp.int32),
+            pltpu.VMEM((2, 160, WIDE), F32),
+            pltpu.VMEM((2, 160, WIDE), F32),
+            pltpu.VMEM((CHUNKS, 4, 8, CHUNK), F32),
+            pltpu.VMEM((4, 2, CHUNKS, 40, 256), F32),
+            pltpu.VMEM((3, 2, CHUNKS, 48, 128), jnp.int32),
+            pltpu.VMEM((3, 2, CHUNKS, 48, 128), jnp.int32),
             pltpu.VMEM((CHUNKS, 48, 128), jnp.int32),
             pltpu.VMEM((CHUNKS, 40, 256), F32),
             pltpu.VMEM((CHUNKS, 48, 128), jnp.int32),
-            pltpu.SemaphoreType.DMA((3,)),
+            pltpu.SemaphoreType.DMA((7,)),
             pltpu.SemaphoreType.DMA((2,)),
             pltpu.SemaphoreType.DMA((5,)),
             pltpu.SemaphoreType.DMA((5,)),
-            pltpu.SemaphoreType.DMA((3, CHUNKS)),
-            pltpu.SemaphoreType.DMA((3, CHUNKS)),
+            pltpu.SemaphoreType.DMA((3, 2, CHUNKS)),
+            pltpu.SemaphoreType.DMA((3, 2, CHUNKS)),
             pltpu.SemaphoreType.DMA((CHUNKS,)),
             pltpu.SemaphoreType.DMA((CHUNKS,)),
             pltpu.SemaphoreType.REGULAR,
         ],
         compiler_params=pltpu.CompilerParams(
-            collective_id=0, has_side_effects=True, vmem_limit_bytes=60 * 2**20
+            collective_id=0, has_side_effects=True, vmem_limit_bytes=48 * 2**20
         ),
     )(
-        model.reshape(20, 4, COARSE),
-        truth.reshape(320, WIDE),
-        climate.reshape(160, WIDE),
-        starts,
-        lat_w.T,
-        lon_first,
-        lon_w,
+        *(
+            pltpu.with_memory_space_constraint(operand, pltpu.HBM)
+            for operand in (
+                model.reshape(20, 4, COARSE),
+                truth.reshape(320, WIDE),
+                climate.reshape(160, WIDE),
+                starts,
+                lat_w.T,
+                lon_first,
+                lon_w,
+            )
+        )
     )
     return maps[0].reshape(2, 5, 1, WIDE), maps[1].reshape(2, 5, 1, WIDE)
 

time: 40.1 us -> 36.2 us (0.903)
  the two profiles are of different devices: /device:TPU:1 before, /device:TPU:56 now
where the time goes in v3:
time: 36.2 us; the launch traced here: 36 us
  Pallas kernels  34.7 us (96%)
  local copies, waits for them, and re-layouts  0.66 us (2%)
  between operations  0.64 us (2%)
    pallas_call x1, Pallas kernels, shards(): pl.pallas_call(kernel, out_shape=jax.ShapeDtypeStruct((2, 10, 1, WIDE), F...  34.7 us

profile of v3, /device:TPU:56, one launch (start us, length us, event | category | flops | bytes accessed | tf_op | source)
XLA Modules:
  0.0 36.0 jit_solution(2635074669714946649)
XLA Ops:
  0.6 34.7 %shard_map.86 = f32[2,10,1,1440]{3,2,1,0:T(1,128)S(1)} custom-call(bf16[20,4,360]{2,1,0:T(4,128)(2,1)} %bitcast.8, bf16[320,1440]{1,0:T(8,128)(2,1)} %bitcast.6, bf16[160,1440]{1,0:T(8,128)(2,1)} %bitcast.7, s32[16]{0:T(128)} %starts_in.1, f32[4,16]{1,0:T(4,128)} %bitcast.11, s32[1440]{0:T(1024)} %lon_first_in.1, bf16[4,1440]{1,0:T(4,128)(2,1)} %lon_w_in.1), custom_call_target="tpu_custom_call" | custom-call | tf_op jit(solution)/shard_map/pallas_call | solution.py:386
  35.4 0.7 %fusion = (f32[1,10,1,1440]{3,2,1,0:T(1,128)}, f32[1,10,1,1440]{3,2,1,0:T(1,128)}) fusion(f32[2,10,1,1440]{3,2,1,0:T(1,128)S(1)} %shard_map.86), kind=kLoop, calls=%fused_computation | loop fusion | bytes 230400 | tf_op jit(solution)/shard_map/slice | solution.py:440

commit v4 on v3

--- a/solution.py
+++ b/solution.py
@@ -290,17 +290,15 @@
         return jnp.concatenate(rows, axis=0)
 
     def hand_over(which, rows, ch):
-        copies = []
-        for k in range(3):
+        copies = {}
+        for k in (1, 0, 2):
             xsend[k, which, ch] = coded(parts[(x + k + 1) % 4, rows, ch])
-            copies.append(
-                send(
-                    xsend.at[k, which, ch],
-                    xrecv.at[k, which, ch],
-                    xssem.at[k, which, ch],
-                    xrsem.at[k, which, ch],
-                    across[k],
-                )
+            copies[k] = send(
+                xsend.at[k, which, ch],
+                xrecv.at[k, which, ch],
+                xssem.at[k, which, ch],
+                xrsem.at[k, which, ch],
+                across[k],
             )
         return copies
 
@@ -340,8 +338,6 @@
                     parts[xx, z, ch, 8 * i : 8 * i + 8] = value[:, 0:256]
                     parts[xx, z, ch, 16 + 8 * i : 24 + 8 * i, 0 : width - 256] = value[:, 256:width]
         first.append(hand_over(0, going, ch))
-    for ch in range(CHUNKS):
-        second.append(hand_over(1, staying, ch))
 
     zcopies = []
     for ch in range(CHUNKS):
@@ -349,6 +345,9 @@
         if ch == 0:
             pl.when(half == 0)(lambda: pl.semaphore_wait(far_in, 1))
         zcopies.append(send(zsend.at[ch], zrecv.at[ch], zssem.at[ch], zrsem.at[ch], far))
+
+    for ch in range(CHUNKS):
+        second.append(hand_over(1, staying, ch))
 
     for ch in range(CHUNKS):
         zown[ch] = collect(1, staying, ch, second[ch])

time: 36.2 us -> 34.2 us (0.945)
  the two profiles are of different devices: /device:TPU:56 before, /device:TPU:34 now
where the time goes in v4:
time: 34.2 us; the launch traced here: 34.1 us
  Pallas kernels  32.8 us (96%)
  local copies, waits for them, and re-layouts  0.66 us (2%)
  between operations  0.64 us (2%)
    pallas_call x1, Pallas kernels, shards(): pl.pallas_call(kernel, out_shape=jax.ShapeDtypeStruct((2, 10, 1, WIDE), F...  32.8 us

profile of v4, /device:TPU:34, one launch (start us, length us, event | category | flops | bytes accessed | tf_op | source)
XLA Modules:
  0.0 34.1 jit_solution(15164782210509027930)
XLA Ops:
  0.6 32.8 %shard_map.86 = f32[2,10,1,1440]{3,2,1,0:T(1,128)S(1)} custom-call(bf16[20,4,360]{2,1,0:T(4,128)(2,1)} %bitcast.8, bf16[320,1440]{1,0:T(8,128)(2,1)} %bitcast.6, bf16[160,1440]{1,0:T(8,128)(2,1)} %bitcast.7, s32[16]{0:T(128)} %starts_in.1, f32[4,16]{1,0:T(4,128)} %bitcast.11, s32[1440]{0:T(1024)} %lon_first_in.1, bf16[4,1440]{1,0:T(4,128)(2,1)} %lon_w_in.1), custom_call_target="tpu_custom_call" | custom-call | tf_op jit(solution)/shard_map/pallas_call | solution.py:385
  33.4 0.7 %fusion = (f32[1,10,1,1440]{3,2,1,0:T(1,128)}, f32[1,10,1,1440]{3,2,1,0:T(1,128)}) fusion(f32[2,10,1,1440]{3,2,1,0:T(1,128)S(1)} %shard_map.86), kind=kLoop, calls=%fused_computation | loop fusion | bytes 230400 | tf_op jit(solution)/shard_map/slice | solution.py:439

commit v5 on v4

--- a/solution.py
+++ b/solution.py
@@ -12,8 +12,8 @@
 BF16 = jnp.bfloat16
 WIDE = 1440
 COARSE = 360
-CHUNK = 512
 CHUNKS = 3
+SPANS = ((0, 512, 256), (512, 1024, 256), (1024, 1440, 256))
 
 
 def upper_rows():
@@ -27,6 +27,7 @@
         most = functools.reduce(jnp.maximum, [jnp.abs(t) for t in tiles])
         more = functools.reduce(jnp.maximum, [jnp.abs(t) for t in tails])
         most = jnp.maximum(jnp.maximum(most, jnp.where(keep, more, 0.0)), 1e-25)
+        most = jnp.max(most, axis=0, keepdims=True)
         return jnp.ceil(jnp.log(most) * (8.0 / 0.6931471805599453) + 0.01)
 
     e_sq, e_an = scale(sqs, upper), scale(ans, jnp.logical_not(upper))
@@ -35,6 +36,9 @@
     words = []
     for tiles, up in ((sqs, up_sq), (ans, up_an), (tails, up_tail)):
         codes = [jnp.round(t * up).astype(jnp.int32) for t in tiles]
+        if len(codes) % 2:
+            odd = codes.pop()
+            codes += [odd[0:4], odd[4:8]]
         for low, high in zip(codes[0::2], codes[1::2], strict=True):
             words.append((high << 16) | (low & 0xFFFF))
     words.append((e_sq.astype(jnp.int32) << 16) | (e_an.astype(jnp.int32) & 0xFFFF))
@@ -42,20 +46,23 @@
 
 
 def decode(words, n, n_tail):
-    count = words.shape[0] // 8
-    tiles = [words[8 * i : 8 * i + 8] for i in range(count)]
-
     def both(t):
         return ((t << 16) >> 16).astype(F32), (t >> 16).astype(F32)
 
-    e_an, e_sq = both(tiles[-1])
+    last = words.shape[0] - 1
+    e_an, e_sq = both(words[last : last + 1])
     down_sq, down_an = (jnp.exp2(e * 0.125) * (1.0 / 32767.0) for e in (e_sq, e_an))
     down_tail = jnp.where(upper_rows(), down_sq, down_an)
     values = []
-    for i, t in enumerate(tiles[:-1]):
-        down = down_sq if i < n // 2 else down_an if i < n else down_tail
-        values += [v * down for v in both(t)]
-    return values[:n], values[n : 2 * n], values[2 * n :]
+    for i in range(n):
+        down = down_sq if i < n // 2 else down_an
+        values += [v * down for v in both(words[8 * i : 8 * i + 8])]
+    tails = []
+    for i in range(n, n + n_tail // 2):
+        tails += [v * down_tail for v in both(words[8 * i : 8 * i + 8])]
+    if n_tail % 2:
+        tails.append(jnp.concatenate(both(words[last - 4 : last]), axis=0) * down_tail)
+    return values[:n], values[n:], tails
 
 
 def kernel(
@@ -164,8 +171,8 @@
         copy.wait()
     first_all = lon_first[...].reshape(1, WIDE)
     weights_all = lon_w[...].astype(F32)
-    for start in range(0, WIDE, CHUNK):
-        width = min(CHUNK, WIDE - start)
+    for start in range(0, WIDE, 512):
+        width = min(512, WIDE - start)
         first = first_all[:, start : start + width]
         step = lax.broadcasted_iota(jnp.int32, (384, width), 0) - first
         step = jnp.where(step < 0, step + COARSE, step)
@@ -187,8 +194,10 @@
     pick_c[...] = (column == target).astype(F32).astype(BF16)
     column = lax.broadcasted_iota(jnp.int32, (160, 320), 1)
     pick[...] = (column == d_of * 160 + target).astype(F32).astype(BF16)
-    mixed[CHUNKS - 1, :, :, 384:512] = jnp.zeros((4, 8, 128), F32)
-    parts[:, :, CHUNKS - 1, 16:32, 128:256] = jnp.zeros((4, 2, 16, 128), F32)
+    for ch, (lo, hi, side) in enumerate(SPANS):
+        if hi - lo < 2 * side:
+            mixed[ch][:, :, side:] = jnp.zeros((4, 8, side), F32)
+            parts[ch][:, :, 16:32] = jnp.zeros((4, 2, 16, side), F32)
 
     stencil = {}
     for xx in range(4):
@@ -203,7 +212,7 @@
             for j in range(5):
                 stencil[xx, z, base + j] = five[j]
 
-    spans = [(lo, min(lo + CHUNK, WIDE)) for lo in range(0, WIDE, CHUNK)]
+    spans = [(lo, min(lo + 512, WIDE)) for lo in range(0, WIDE, 512)]
     own_climate.wait()
     own_truth.wait()
     for s in range(2):
@@ -274,10 +283,9 @@
             put(128 + 16 * pairx, jnp.concatenate(pieces, axis=0))
 
     going, staying = 1 - half, half
-    even = lax.broadcasted_iota(jnp.int32, (8, 256), 0) % 4 < 2
 
     def coded(block):
-        tiles = [block[:, 0:128], block[:, 128:256]]
+        tiles = [block[:, j : j + 128] for j in range(0, block.shape[1], 128)]
         return encode(
             [t[r : r + 8] for r in (0, 16) for t in tiles],
             [t[r : r + 8] for r in (8, 24) for t in tiles],
@@ -285,17 +293,18 @@
         )
 
     def plain(words):
-        sqs, ans, tails = decode(words, 4, 2)
-        rows = [jnp.concatenate(g, axis=1) for g in (sqs[0:2], ans[0:2], sqs[2:4], ans[2:4], tails)]
+        n = words.shape[0] // 20
+        sqs, ans, tails = decode(words, 2 * n, n)
+        rows = [jnp.concatenate(g, axis=1) for g in (sqs[:n], ans[:n], sqs[n:], ans[n:], tails)]
         return jnp.concatenate(rows, axis=0)
 
     def hand_over(which, rows, ch):
         copies = {}
         for k in (1, 0, 2):
-            xsend[k, which, ch] = coded(parts[(x + k + 1) % 4, rows, ch])
+            xsend[ch][k, which] = coded(parts[ch][(x + k + 1) % 4, rows])
             copies[k] = send(
-                xsend.at[k, which, ch],
-                xrecv.at[k, which, ch],
+                xsend[ch].at[k, which],
+                xrecv[ch].at[k, which],
                 xssem.at[k, which, ch],
                 xrsem.at[k, which, ch],
                 across[k],
@@ -303,15 +312,16 @@
         return copies
 
     def collect(which, rows, ch, copies):
-        total = parts[x, rows, ch]
+        total = parts[ch][x, rows]
         for k in range(3):
             copies[k].wait_recv()
-            total += plain(xrecv[k, which, ch])
+            total += plain(xrecv[ch][k, which])
         return total
 
     first, second = [], []
-    for ch, (lo, hi) in enumerate(spans):
+    for ch, (lo, hi, side) in enumerate(SPANS):
         width = hi - lo
+        even = lax.broadcasted_iota(jnp.int32, (8, side), 0) % 4 < 2
         w = table[:, lo:hi]
         sq = an = None
         for s in range(2):
@@ -327,37 +337,37 @@
         for xx in range(4):
             tail = slice(128 + 8 * xx, 136 + 8 * xx)
             both = [t + pltpu.roll(t, 4, 0) for t in (sq[tail], an[tail])]
-            mixed[ch, xx, :, 0:width] = jnp.where(upper, both[0], both[1])
-            left, right = mixed[ch, xx, :, 0:256], mixed[ch, xx, :, 256:512]
-            parts[xx, 0, ch, 32:40] = jnp.where(even, left, pltpu.roll(right, 2, 0))
-            parts[xx, 1, ch, 32:40] = jnp.where(even, pltpu.roll(left, 6, 0), right)
+            mixed[ch][xx, :, 0:width] = jnp.where(upper, both[0], both[1])
+            left, right = mixed[ch][xx, :, 0:side], mixed[ch][xx, :, side:]
+            parts[ch][xx, 0, 32:40] = jnp.where(even, left, pltpu.roll(right, 2, 0))
+            parts[ch][xx, 1, 32:40] = jnp.where(even, pltpu.roll(left, 6, 0), right)
             for z in range(2):
                 r = 16 * xx + 8 * z
                 for i, t in enumerate((sq, an)):
                     value = t[r : r + 8] + t[64 + r : 72 + r]
-                    parts[xx, z, ch, 8 * i : 8 * i + 8] = value[:, 0:256]
-                    parts[xx, z, ch, 16 + 8 * i : 24 + 8 * i, 0 : width - 256] = value[:, 256:width]
+                    parts[ch][xx, z, 8 * i : 8 * i + 8] = value[:, 0:side]
+                    parts[ch][xx, z, 16 + 8 * i : 24 + 8 * i, 0 : width - side] = value[:, side:width]
         first.append(hand_over(0, going, ch))
 
     zcopies = []
     for ch in range(CHUNKS):
-        zsend[ch] = coded(collect(0, going, ch, first[ch]))
+        zsend[ch][...] = coded(collect(0, going, ch, first[ch]))
         if ch == 0:
             pl.when(half == 0)(lambda: pl.semaphore_wait(far_in, 1))
-        zcopies.append(send(zsend.at[ch], zrecv.at[ch], zssem.at[ch], zrsem.at[ch], far))
+        zcopies.append(send(zsend[ch], zrecv[ch], zssem.at[ch], zrsem.at[ch], far))
 
     for ch in range(CHUNKS):
         second.append(hand_over(1, staying, ch))
 
     for ch in range(CHUNKS):
-        zown[ch] = collect(1, staying, ch, second[ch])
-
-    for ch, (start, _) in enumerate(spans):
+        zown[ch][...] = collect(1, staying, ch, second[ch])
+
+    for ch, (start, stop, half_width) in enumerate(SPANS):
         zcopies[ch].wait_recv()
-        total = (zown[ch] + plain(zrecv[ch])) * (1.0 / 32.0)
+        total = (zown[ch][...] + plain(zrecv[ch][...])) * (1.0 / 32.0)
         for side in range(2):
-            lo = start + side * 256
-            hi = min(lo + 256, WIDE)
+            lo = start + side * half_width
+            hi = min(lo + half_width, stop)
             width = hi - lo
             for which in range(2):
                 r = 16 * side + 8 * which
@@ -377,6 +387,10 @@
     def _():
         edges[1].wait_send()
         edges[3].wait_send()
+
+
+def per_chunk(buffer):
+    return [buffer(side, 20 * (side // 128) + 1) for _, _, side in SPANS]
 
 
 def shards(model, truth, climate, starts, lat_w, lon_first, lon_w):
@@ -402,13 +416,13 @@
             pltpu.VMEM((160, 160), BF16),
             pltpu.VMEM((2, 160, WIDE), F32),
             pltpu.VMEM((2, 160, WIDE), F32),
-            pltpu.VMEM((CHUNKS, 4, 8, CHUNK), F32),
-            pltpu.VMEM((4, 2, CHUNKS, 40, 256), F32),
-            pltpu.VMEM((3, 2, CHUNKS, 48, 128), jnp.int32),
-            pltpu.VMEM((3, 2, CHUNKS, 48, 128), jnp.int32),
-            pltpu.VMEM((CHUNKS, 48, 128), jnp.int32),
-            pltpu.VMEM((CHUNKS, 40, 256), F32),
-            pltpu.VMEM((CHUNKS, 48, 128), jnp.int32),
+            per_chunk(lambda side, rows: pltpu.VMEM((4, 8, 2 * side), F32)),
+            per_chunk(lambda side, rows: pltpu.VMEM((4, 2, 40, side), F32)),
+            per_chunk(lambda side, rows: pltpu.VMEM((3, 2, rows, 128), jnp.int32)),
+            per_chunk(lambda side, rows: pltpu.VMEM((3, 2, rows, 128), jnp.int32)),
+            per_chunk(lambda side, rows: pltpu.VMEM((rows, 128), jnp.int32)),
+            per_chunk(lambda side, rows: pltpu.VMEM((40, side), F32)),
+            per_chunk(lambda side, rows: pltpu.VMEM((rows, 128), jnp.int32)),
             pltpu.SemaphoreType.DMA((7,)),
             pltpu.SemaphoreType.DMA((2,)),
             pltpu.SemaphoreType.DMA((5,)),

time: 34.2 us -> 32.8 us (0.959)
  the two profiles are of different devices: /device:TPU:34 before, /device:TPU:1 now
where the time goes in v5:
time: 32.8 us; the launch traced here: 32.6 us
  Pallas kernels  31.3 us (95%)
  local copies, waits for them, and re-layouts  0.66 us (2%)
  between operations  0.64 us (2%)
    pallas_call x1, Pallas kernels, shards(): pl.pallas_call(kernel, out_shape=jax.ShapeDtypeStruct((2, 10, 1, WIDE), F...  31.3 us
    slice x1, local copies, waits for them, and re-layouts, shards(): return (maps[0].reshape(2, 5, 1, WIDE), maps[1].reshape(2, 5, 1, WIDE))  0.66 us

profile of v5, /device:TPU:1, one launch (start us, length us, event | category | flops | bytes accessed | tf_op | source)
XLA Modules:
  0.0 32.6 jit_solution(9249052589639001568)
XLA Ops:
  0.6 31.3 %shard_map.86 = f32[2,10,1,1440]{3,2,1,0:T(1,128)S(1)} custom-call(bf16[20,4,360]{2,1,0:T(4,128)(2,1)} %bitcast.8, bf16[320,1440]{1,0:T(8,128)(2,1)} %bitcast.6, bf16[160,1440]{1,0:T(8,128)(2,1)} %bitcast.7, s32[16]{0:T(128)} %starts_in.1, f32[4,16]{1,0:T(4,128)} %bitcast.11, s32[1440]{0:T(1024)} %lon_first_in.1, bf16[4,1440]{1,0:T(4,128)(2,1)} %lon_w_in.1), custom_call_target="tpu_custom_call" | custom-call | tf_op jit(solution)/shard_map/pallas_call | solution.py:399
  32.0 0.7 %fusion = (f32[1,10,1,1440]{3,2,1,0:T(1,128)}, f32[1,10,1,1440]{3,2,1,0:T(1,128)}) fusion(f32[2,10,1,1440]{3,2,1,0:T(1,128)S(1)} %shard_map.86), kind=kLoop, calls=%fused_computation | loop fusion | bytes 230400 | tf_op jit(solution)/shard_map/slice | solution.py:453

commit v6 on v5

--- a/solution.py
+++ b/solution.py
@@ -68,7 +68,7 @@
 def kernel(
     model, truth, climate, starts_in, lat_w_in, lon_first_in, lon_w_in,
     out,
-    starts, lat_w, lon_first, lon_w, mbuf, tbuf, cbuf, crs, fields, table, pick, pick_c, actual, anomaly, mixed, parts, xsend, xrecv, zsend, zown, zrecv,
+    starts, lat_w, lon_first, lon_w, mbuf, tbuf, cbuf, crs, fields, table, pick, pick_c, inner, actual, anomaly, mixed, parts, xsend, xrecv, zsend, zown, zrecv,
     lsem, tsem, csend, crecv, xssem, xrsem, zssem, zrsem, far_in,
 ):
     date = lax.axis_index("date")
@@ -224,6 +224,40 @@
             actual[s, :, lo:hi] = t
             anomaly[s, :, lo:hi] = t - clim
 
+    zmask = (lax.broadcasted_iota(jnp.int32, (8, 384), 0) // 2) % 2 == 0
+
+    def stencil_sum(s, pairs):
+        planes = {}
+        for pair in pairs:
+            both = crs[s, pair].astype(F32)
+            planes[2 * pair], planes[2 * pair + 1] = both[0:24], both[24:48]
+
+        def weigh(terms):
+            terms = [w * v for w, v in terms]
+            return functools.reduce(jnp.add, terms) if terms else None
+
+        result = {}
+        for xx in range(4):
+            for d in range(2):
+                for z in range(2):
+                    reach = range(2 * z + xx // 2, 2 * z + xx // 2 + 5)
+                    result[d * 64 + xx * 16 + z * 8] = weigh(
+                        [(stencil[xx, z, c], planes[c][8 * d : 8 * d + 8]) for c in reach if c in planes]
+                    )
+            terms = []
+            for c in planes:
+                w0, w1 = stencil.get((xx, 0, c)), stencil.get((xx, 1, c))
+                if w0 is not None or w1 is not None:
+                    w = jnp.where(zmask, 0.0 if w0 is None else w0, 0.0 if w1 is None else w1)
+                    terms.append((w, planes[c][16:24]))
+            result[128 + 8 * xx] = weigh(terms)
+        return result
+
+    swap.wait_recv()
+    for s in range(2):
+        for r, value in stencil_sum(s, (1, 2)).items():
+            inner[s, r : r + 8] = value
+
     @pl.when(not_first)
     def _():
         edges[0].wait_recv()
@@ -242,45 +276,16 @@
     def _():
         crs[:, 3] = jnp.zeros((2, 48, 384), BF16)
 
-    swap.wait_recv()
-    zmask = (lax.broadcasted_iota(jnp.int32, (8, 384), 0) // 2) % 2 == 0
     for s in range(2):
-        planes = []
-        for pair in range(4):
-            both = crs[s, pair].astype(F32)
-            planes += [both[0:24], both[24:48]]
-
-        def put(at_row, value):
+        edge = stencil_sum(s, (0, 3))
+        for r in range(0, 160, 16):
+            rows = []
+            for q in (r, r + 8):
+                rows.append(inner[s, q : q + 8] if edge[q] is None else inner[s, q : q + 8] + edge[q])
+            value = jnp.concatenate(rows, axis=0)
             high = value.astype(BF16)
-            low = (value - high.astype(F32)).astype(BF16)
-            rows = value.shape[0]
-            fields[0, s, at_row : at_row + rows, :] = high
-            fields[1, s, at_row : at_row + rows, :] = low
-
-        for d in range(2):
-            for xx in range(4):
-                pieces = []
-                for z in range(2):
-                    total = None
-                    for j in range(5):
-                        c = 2 * z + xx // 2 + j
-                        term = stencil[xx, z, c] * planes[c][8 * d : 8 * d + 8]
-                        total = term if total is None else total + term
-                    pieces.append(total)
-                put(d * 64 + xx * 16, jnp.concatenate(pieces, axis=0))
-        for pairx in range(2):
-            pieces = []
-            for xx in (2 * pairx, 2 * pairx + 1):
-                total = None
-                for c in range(8):
-                    w0, w1 = stencil.get((xx, 0, c)), stencil.get((xx, 1, c))
-                    if w0 is None and w1 is None:
-                        continue
-                    w = jnp.where(zmask, 0.0 if w0 is None else w0, 0.0 if w1 is None else w1)
-                    term = w * planes[c][16:24]
-                    total = term if total is None else total + term
-                pieces.append(total)
-            put(128 + 16 * pairx, jnp.concatenate(pieces, axis=0))
+            fields[0, s, r : r + 16] = high
+            fields[1, s, r : r + 16] = (value - high.astype(F32)).astype(BF16)
 
     going, staying = 1 - half, half
 
@@ -300,8 +305,10 @@
 
     def hand_over(which, rows, ch):
         copies = {}
+        messages = [coded(parts[ch][(x + k + 1) % 4, rows]) for k in range(3)]
+        for k in range(3):
+            xsend[ch][k, which] = messages[k]
         for k in (1, 0, 2):
-            xsend[ch][k, which] = coded(parts[ch][(x + k + 1) % 4, rows])
             copies[k] = send(
                 xsend[ch].at[k, which],
                 xrecv[ch].at[k, which],
@@ -414,6 +421,7 @@
             pltpu.VMEM((384, WIDE), BF16),
             pltpu.VMEM((160, 320), BF16),
             pltpu.VMEM((160, 160), BF16),
+            pltpu.VMEM((2, 160, 384), F32),
             pltpu.VMEM((2, 160, WIDE), F32),
             pltpu.VMEM((2, 160, WIDE), F32),
             per_chunk(lambda side, rows: pltpu.VMEM((4, 8, 2 * side), F32)),

time: 32.8 us -> 32.7 us (level)
  the two profiles are of different devices: /device:TPU:1 before, /device:TPU:32 now
where the time goes in v6:
time: 32.7 us; the launch traced here: 32.5 us
  Pallas kernels  31.2 us (95%)
  local copies, waits for them, and re-layouts  0.66 us (2%)
  between operations  0.64 us (2%)
    pallas_call x1, Pallas kernels, shards(): pl.pallas_call(kernel, out_shape=jax.ShapeDtypeStruct((2, 10, 1, WIDE), F...  31.2 us
    slice x1, local copies, waits for them, and re-layouts, shards(): return (maps[0].reshape(2, 5, 1, WIDE), maps[1].reshape(2, 5, 1, WIDE))  0.66 us

profile of v6, /device:TPU:32, one launch (start us, length us, event | category | flops | bytes accessed | tf_op | source)
XLA Modules:
  0.0 32.5 jit_solution(7716616742128402553)
XLA Ops:
  0.6 31.2 %shard_map.86 = f32[2,10,1,1440]{3,2,1,0:T(1,128)S(1)} custom-call(bf16[20,4,360]{2,1,0:T(4,128)(2,1)} %bitcast.8, bf16[320,1440]{1,0:T(8,128)(2,1)} %bitcast.6, bf16[160,1440]{1,0:T(8,128)(2,1)} %bitcast.7, s32[16]{0:T(128)} %starts_in.1, f32[4,16]{1,0:T(4,128)} %bitcast.11, s32[1440]{0:T(1024)} %lon_first_in.1, bf16[4,1440]{1,0:T(4,128)(2,1)} %lon_w_in.1), custom_call_target="tpu_custom_call" | custom-call | tf_op jit(solution)/shard_map/pallas_call | solution.py:406
  31.9 0.7 %fusion = (f32[1,10,1,1440]{3,2,1,0:T(1,128)}, f32[1,10,1,1440]{3,2,1,0:T(1,128)}) fusion(f32[2,10,1,1440]{3,2,1,0:T(1,128)S(1)} %shard_map.86), kind=kLoop, calls=%fused_computation | loop fusion | bytes 230400 | tf_op jit(solution)/shard_map/slice | solution.py:461

commit v7 on v6

--- a/solution.py
+++ b/solution.py
@@ -13,7 +13,7 @@
 WIDE = 1440
 COARSE = 360
 CHUNKS = 3
-SPANS = ((0, 512, 256), (512, 1024, 256), (1024, 1440, 256))
+SPANS = ((1024, 1440, 256), (0, 512, 256), (512, 1024, 256))
 
 
 def upper_rows():

time: 32.7 us -> 32.7 us (level)
  no operation moved by 1% of the time
where the time goes in v7:
time: 32.7 us; the launch traced here: 32.5 us
  Pallas kernels  31.2 us (95%)
  local copies, waits for them, and re-layouts  0.66 us (2%)
  between operations  0.64 us (2%)
    pallas_call x1, Pallas kernels, shards(): pl.pallas_call(kernel, out_shape=jax.ShapeDtypeStruct((2, 10, 1, WIDE), F...  31.2 us
    slice x1, local copies, waits for them, and re-layouts, shards(): return (maps[0].reshape(2, 5, 1, WIDE), maps[1].reshape(2, 5, 1, WIDE))  0.66 us

profile of v7, /device:TPU:32, one launch (start us, length us, event | category | flops | bytes accessed | tf_op | source)
XLA Modules:
  0.0 32.5 jit_solution(15917755451121579668)
XLA Ops:
  0.6 31.2 %shard_map.86 = f32[2,10,1,1440]{3,2,1,0:T(1,128)S(1)} custom-call(bf16[20,4,360]{2,1,0:T(4,128)(2,1)} %bitcast.8, bf16[320,1440]{1,0:T(8,128)(2,1)} %bitcast.6, bf16[160,1440]{1,0:T(8,128)(2,1)} %bitcast.7, s32[16]{0:T(128)} %starts_in.1, f32[4,16]{1,0:T(4,128)} %bitcast.11, s32[1440]{0:T(1024)} %lon_first_in.1, bf16[4,1440]{1,0:T(4,128)(2,1)} %lon_w_in.1), custom_call_target="tpu_custom_call" | custom-call | tf_op jit(solution)/shard_map/pallas_call | solution.py:406
  31.9 0.7 %fusion = (f32[1,10,1,1440]{3,2,1,0:T(1,128)}, f32[1,10,1,1440]{3,2,1,0:T(1,128)}) fusion(f32[2,10,1,1440]{3,2,1,0:T(1,128)S(1)} %shard_map.86), kind=kLoop, calls=%fused_computation | loop fusion | bytes 230400 | tf_op jit(solution)/shard_map/slice | solution.py:461
